TPU v7x, 512 devices: a whole 4x8x8 slice. The times are simulated.
512 devices in a mesh: tm: 32 (over y, x), space: 16 (over z, core).
Axes of the slice: x: 4, y: 8, z: 8, core: 2. Of those that a mesh axis runs over, the one named last changes fastest.
Arguments:
- local_term: float32 [32, 512, 512], P('tm', 'space'), may hold values from -2 to 16, as said below
- coupling: float32 [32, 512, 512], P('tm', 'space'), may hold values from -0.25 to 1.2
Outputs:
- sigma: float32 [32, 512, 512], P('tm', 'space')
Inputs may be any that keep to these rules, and one draw needn't show every extreme that they name: local_term[t] is symmetric for every time block t.
All inputs are finite; a program needn't handle non-finite values.
Results may differ from a plain program's by a relative error of at most 0.00014.
Values sent between devices are 32-bit elements; how exact they have to be, the bound alone decides.
No kernel may reach another device: no remote copies, remote signals or barrier semaphores. Data moves between devices by JAX's collectives and lax.ppermute only.
A program may use at most 64 MiB of HBM per device.

v0:
```python
import jax
import jax.numpy as jnp
from jax import lax
from jax.sharding import PartitionSpec as P

HIGH = lax.Precision.HIGHEST


def from_behind(shard, axis, by):
    peers = lax.axis_size(axis)
    pairs = [(i, i + by) for i in range(peers) if 0 <= i + by < peers]
    return lax.ppermute(shard, axis, pairs)


def matmul(left, right):
    return jnp.dot(left, right, precision=HIGH, preferred_element_type=jnp.float32)


def inner_rows(left, right):
    return lax.dot_general(
        left, right, (((0,), (0,)), ((), ())), precision=HIGH, preferred_element_type=jnp.float32
    )


def combine(terms, maps, later_terms, later_maps, owner):
    rows, width = terms.shape

    def accumulate(piece):
        product = matmul(later_terms, piece)
        if later_maps is None:
            return (product,)
        return (product, matmul(later_maps, piece))

    folded = accumulate(lax.all_gather(maps, "space", axis=0, tiled=True))
    weighted = folded[0]
    own_columns = lax.dynamic_slice_in_dim(
        lax.all_gather(maps, "space", axis=0, tiled=True), owner * rows, rows, 1
    )
    congruence = inner_rows(own_columns, lax.all_gather(weighted, "space", axis=0, tiled=True))
    new_terms = terms + congruence
    new_maps = None if later_maps is None else folded[1]
    return (new_terms, new_maps)


def local(local_term, coupling):
    terms = local_term[0]
    maps = coupling[0]
    count_tm = lax.axis_size("tm")
    levels = (count_tm - 1).bit_length()
    owner = lax.axis_index("space")
    for level in range(levels):
        offset = 1 << level
        if level == levels - 1:
            later_terms = from_behind(terms, "tm", -offset)
            later_maps = None
        else:
            later_terms, later_maps = from_behind((terms, maps), "tm", -offset)
        terms, maps = combine(terms, maps, later_terms, later_maps, owner)
    return terms[None]


def solution(mesh):
    placed = (P("tm", "space", None), P("tm", "space", None))
    return jax.shard_map(
        local, mesh=mesh, in_specs=placed, out_specs=P("tm", "space", None), check_vma=False
    )
```

profile of v0, /device:TPU:1, one launch (start us, length us, event | category | flops | bytes accessed | tf_op | source)
XLA Modules:
  0.0 450.1 jit_solution(3637459121479575733)
XLA Ops:
  8.7 4.3 collective-permute-done
  13.0 44.4 %all-gather.30.cloned.1.call-done = f32[1,512,512]{2,1,0:T(8,128)} async-done(((f32[1,32,512]{2,1,0:T(8,128)}), f32[1,512,512]{2,1,0:T(8,128)}) %all-gather.30.cloned.1.call-update) | async-done | bytes 1048592 | tf_op jit(solution)/shard_map/all_gather | solution.py:37
  57.4 2.6 fusion.1
  62.1 3.7 collective-permute-done.1
  67.3 33.0 %all-gather.12.cloned.1.call-done = f32[512,512]{1,0:T(8,128)} async-done(((f32[32,512]{1,0:T(8,128)}), f32[512,512]{1,0:T(8,128)}) %all-gather.12.cloned.1.call-update) | async-done | bytes 1048592 | tf_op jit(solution)/shard_map/all_gather | solution.py:39
  100.3 2.0 convolution_add_fusion.4
  103.5 39.0 %all-gather.14.cloned.1.call-done = f32[512,512]{1,0:T(8,128)} async-done(((f32[32,512]{1,0:T(8,128)}), f32[512,512]{1,0:T(8,128)}) %all-gather.14.cloned.1.call-update) | async-done | bytes 1048592 | tf_op jit(solution)/shard_map/all_gather | solution.py:37
  142.5 2.6 fusion.16
  147.3 5.2 %collective-permute-done.3 = f32[32,512]{1,0:T(8,128)S(1)} collective-permute-done((f32[32,512]{1,0:T(8,128)S(1)}, f32[32,512]{1,0:T(8,128)S(1)}, u32[]{:S(2)}, u32[]{:S(2)}) %collective-permute-start.3) | collective-permute-done | bytes 65568 | tf_op jit(solution)/shard_map/ppermute | solution.py:12
  153.9 31.5 %all-gather.16.cloned.1.call-done = f32[512,512]{1,0:T(8,128)} async-done(((f32[32,512]{1,0:T(8,128)}), f32[512,512]{1,0:T(8,128)}) %all-gather.16.cloned.1.call-update) | async-done | bytes 1048592 | tf_op jit(solution)/shard_map/all_gather | solution.py:39
  185.4 2.0 convolution_add_fusion.3
  188.7 38.8 %all-gather.18.cloned.1.call-done = f32[512,512]{1,0:T(8,128)} async-done(((f32[32,512]{1,0:T(8,128)}), f32[512,512]{1,0:T(8,128)}) %all-gather.18.cloned.1.call-update) | async-done | bytes 1048592 | tf_op jit(solution)/shard_map/all_gather | solution.py:37
  227.5 2.6 fusion.18
  232.3 3.7 collective-permute-done.5
  237.4 33.0 %all-gather.20.cloned.1.call-done = f32[512,512]{1,0:T(8,128)} async-done(((f32[32,512]{1,0:T(8,128)}), f32[512,512]{1,0:T(8,128)}) %all-gather.20.cloned.1.call-update) | async-done | bytes 1048592 | tf_op jit(solution)/shard_map/all_gather | solution.py:39
  270.4 2.0 convolution_add_fusion.2
  273.7 39.0 %all-gather.22.cloned.1.call-done = f32[512,512]{1,0:T(8,128)} async-done(((f32[32,512]{1,0:T(8,128)}), f32[512,512]{1,0:T(8,128)}) %all-gather.22.cloned.1.call-update) | async-done | bytes 1048592 | tf_op jit(solution)/shard_map/all_gather | solution.py:37
  312.6 2.6 fusion.20
  317.4 4.6 %collective-permute-done.7 = f32[32,512]{1,0:T(8,128)S(1)} collective-permute-done((f32[32,512]{1,0:T(8,128)S(1)}, f32[32,512]{1,0:T(8,128)S(1)}, u32[]{:S(2)}, u32[]{:S(2)}) %collective-permute-start.7) | collective-permute-done | bytes 65568 | tf_op jit(solution)/shard_map/ppermute | solution.py:12
  323.4 32.1 %all-gather.24.cloned.1.call-done = f32[512,512]{1,0:T(8,128)} async-done(((f32[32,512]{1,0:T(8,128)}), f32[512,512]{1,0:T(8,128)}) %all-gather.24.cloned.1.call-update) | async-done | bytes 1048592 | tf_op jit(solution)/shard_map/all_gather | solution.py:39
  358.8 39.0 %all-gather.26.cloned.1.call-done = f32[512,512]{1,0:T(8,128)} async-done(((f32[32,512]{1,0:T(8,128)}), f32[512,512]{1,0:T(8,128)}) %all-gather.26.cloned.1.call-update) | async-done | bytes 1048592 | tf_op jit(solution)/shard_map/all_gather | solution.py:37
  397.8 2.6 fusion.22
  400.3 40.2 %all-gather.28.cloned.1.call-done = f32[512,512]{1,0:T(8,128)} async-done(((f32[32,512]{1,0:T(8,128)}), f32[512,512]{1,0:T(8,128)}) %all-gather.28.cloned.1.call-update) | async-done | bytes 1048592 | tf_op jit(solution)/shard_map/all_gather | solution.py:39
  440.6 2.7 fusion
  (56 shorter events, 23.2 us)
Async XLA Ops:
  6.5 0.8 copy-start.8
  6.5 50.8 %all-gather.30.cloned.1.call-start = ((), (), s32[]{:S(2)}) async-start(), calls=%async_computation.9 | async-start | bytes 1114112 | tf_op jit(solution)/shard_map/all_gather | solution.py:37
  7.3 93.0 %all-gather.12.cloned.1.call-start = ((), (), s32[]{:S(2)}) async-start(), calls=%async_computation | async-start | bytes 1114112 | tf_op jit(solution)/shard_map/all_gather | solution.py:39
  7.4 5.6 %collective-permute-start = (f32[32,512]{1,0:T(8,128)S(1)}, f32[32,512]{1,0:T(8,128)S(1)}, u32[]{:S(2)}, u32[]{:S(2)}) collective-permute-start(f32[32,512]{1,0:T(8,128)S(1)} %bitcast.35), channel_id=1, source_target_pairs={{16,0},{32,16},{48,32},{64,48},{80,64},{96,80},{112,96},{128,112},... | collective-permute-start | bytes 196616 | tf_op jit(solution)/shard_map/ppermute | solution.py:12
  57.4 8.5 %copy-start.1 = (f32[1,512,512]{2,1,0:T(8,128)S(1)}, f32[1,512,512]{2,1,0:T(8,128)}, u32[]{:S(2)}) copy-start(f32[1,512,512]{2,1,0:T(8,128)} %all-gather.30.cloned.1.call-done) | copy-start | bytes 3145732
  60.0 82.5 %all-gather.14.cloned.1.call-start = ((), (), s32[]{:S(2)}) async-start(), calls=%async_computation.1 | async-start | bytes 1114112 | tf_op jit(solution)/shard_map/all_gather | solution.py:37
  60.9 5.0 %collective-permute-start.1 = (f32[32,512]{1,0:T(8,128)S(1)}, f32[32,512]{1,0:T(8,128)S(1)}, u32[]{:S(2)}, u32[]{:S(2)}) collective-permute-start(f32[32,512]{1,0:T(8,128)S(1)} %bitcast.34), channel_id=1, source_target_pairs={{16,0},{32,16},{48,32},{64,48},{80,64},{96,80},{112,96},{128,112},... | collective-permute-start | bytes 196616 | tf_op jit(solution)/shard_map/ppermute | solution.py:12
  67.2 118.2 %all-gather.16.cloned.1.call-start = ((), (), s32[]{:S(2)}) async-start(), calls=%async_computation.2 | async-start | bytes 1114112 | tf_op jit(solution)/shard_map/all_gather | solution.py:39
  102.2 40.3 %collective-permute-start.2 = (f32[32,512]{1,0:T(8,128)S(1)}, f32[32,512]{1,0:T(8,128)S(1)}, u32[]{:S(2)}, u32[]{:S(2)}) collective-permute-start(f32[32,512]{1,0:T(8,128)S(1)} %convolution_add_fusion.4), channel_id=1, source_target_pairs={{32,0},{48,16},{64,32},{80,48},{96,64},{112,80},{128,96},{144,112}... | collective-permute-start | bytes 196616 | tf_op jit(solution)/shard_map/ppermute | solution.py:12
  142.5 10.0 %copy-start = (f32[512,512]{1,0:T(8,128)S(1)}, f32[512,512]{1,0:T(8,128)}, u32[]{:S(2)}) copy-start(f32[512,512]{1,0:T(8,128)} %all-gather.14.cloned.1.call-done) | copy-start | bytes 3145732
  145.2 82.3 %all-gather.18.cloned.1.call-start = ((), (), s32[]{:S(2)}) async-start(), calls=%async_computation.3 | async-start | bytes 1114112 | tf_op jit(solution)/shard_map/all_gather | solution.py:37
  146.0 6.5 %collective-permute-start.3 = (f32[32,512]{1,0:T(8,128)S(1)}, f32[32,512]{1,0:T(8,128)S(1)}, u32[]{:S(2)}, u32[]{:S(2)}) collective-permute-start(f32[32,512]{1,0:T(8,128)S(1)} %copy-done.4), channel_id=1, source_target_pairs={{32,0},{48,16},{64,32},{80,48},{96,64},{112,80},{128,96},{144,112}... | collective-permute-start | bytes 196616 | tf_op jit(solution)/shard_map/ppermute | solution.py:12
  153.8 116.6 %all-gather.20.cloned.1.call-start = ((), (), s32[]{:S(2)}) async-start(), calls=%async_computation.4 | async-start | bytes 1114112 | tf_op jit(solution)/shard_map/all_gather | solution.py:39
  187.4 40.1 %collective-permute-start.4 = (f32[32,512]{1,0:T(8,128)S(1)}, f32[32,512]{1,0:T(8,128)S(1)}, u32[]{:S(2)}, u32[]{:S(2)}) collective-permute-start(f32[32,512]{1,0:T(8,128)S(1)} %convolution_add_fusion.3), channel_id=1, source_target_pairs={{64,0},{80,16},{96,32},{112,48},{128,64},{144,80},{160,96},{176,11... | collective-permute-start | bytes 196616 | tf_op jit(solution)/shard_map/ppermute | solution.py:12
  227.5 8.5 %copy-start.2 = (f32[512,512]{1,0:T(8,128)S(1)}, f32[512,512]{1,0:T(8,128)}, u32[]{:S(2)}) copy-start(f32[512,512]{1,0:T(8,128)} %all-gather.18.cloned.1.call-done) | copy-start | bytes 3145732
  230.2 82.5 %all-gather.22.cloned.1.call-start = ((), (), s32[]{:S(2)}) async-start(), calls=%async_computation.5 | async-start | bytes 1114112 | tf_op jit(solution)/shard_map/all_gather | solution.py:37
  231.0 5.0 %collective-permute-start.5 = (f32[32,512]{1,0:T(8,128)S(1)}, f32[32,512]{1,0:T(8,128)S(1)}, u32[]{:S(2)}, u32[]{:S(2)}) collective-permute-start(f32[32,512]{1,0:T(8,128)S(1)} %copy-done.5), channel_id=1, source_target_pairs={{64,0},{80,16},{96,32},{112,48},{128,64},{144,80},{160,96},{176,11... | collective-permute-start | bytes 196616 | tf_op jit(solution)/shard_map/ppermute | solution.py:12
  237.3 118.2 %all-gather.24.cloned.1.call-start = ((), (), s32[]{:S(2)}) async-start(), calls=%async_computation.6 | async-start | bytes 1114112 | tf_op jit(solution)/shard_map/all_gather | solution.py:39
  272.4 40.3 %collective-permute-start.6 = (f32[32,512]{1,0:T(8,128)S(1)}, f32[32,512]{1,0:T(8,128)S(1)}, u32[]{:S(2)}, u32[]{:S(2)}) collective-permute-start(f32[32,512]{1,0:T(8,128)S(1)} %convolution_add_fusion.2), channel_id=1, source_target_pairs={{128,0},{144,16},{160,32},{176,48},{192,64},{208,80},{224,96},{240... | collective-permute-start | bytes 196616 | tf_op jit(solution)/shard_map/ppermute | solution.py:12
  312.6 9.4 %copy-start.3 = (f32[512,512]{1,0:T(8,128)S(1)}, f32[512,512]{1,0:T(8,128)}, u32[]{:S(2)}) copy-start(f32[512,512]{1,0:T(8,128)} %all-gather.22.cloned.1.call-done) | copy-start | bytes 3145732
  315.3 82.5 %all-gather.26.cloned.1.call-start = ((), (), s32[]{:S(2)}) async-start(), calls=%async_computation.7 | async-start | bytes 1114112 | tf_op jit(solution)/shard_map/all_gather | solution.py:37
  316.1 5.9 %collective-permute-start.7 = (f32[32,512]{1,0:T(8,128)S(1)}, f32[32,512]{1,0:T(8,128)S(1)}, u32[]{:S(2)}, u32[]{:S(2)}) collective-permute-start(f32[32,512]{1,0:T(8,128)S(1)} %copy-done.6), channel_id=1, source_target_pairs={{128,0},{144,16},{160,32},{176,48},{192,64},{208,80},{224,96},{240... | collective-permute-start | bytes 196616 | tf_op jit(solution)/shard_map/ppermute | solution.py:12
  323.4 117.2 %all-gather.28.cloned.1.call-start = ((), (), s32[]{:S(2)}) async-start(), calls=%async_computation.8 | async-start | bytes 1114112 | tf_op jit(solution)/shard_map/all_gather | solution.py:39
  357.5 40.3 %collective-permute-start.8 = (f32[32,512]{1,0:T(8,128)S(1)}, f32[32,512]{1,0:T(8,128)S(1)}, u32[]{:S(2)}, u32[]{:S(2)}) collective-permute-start(f32[32,512]{1,0:T(8,128)S(1)} %convolution_add_fusion.1), channel_id=1, source_target_pairs={{256,0},{272,16},{288,32},{304,48},{320,64},{336,80},{352,96},{368... | collective-permute-start | bytes 196616 | tf_op jit(solution)/shard_map/ppermute | solution.py:12
  (4 other events, 3.4 us)
Sparse Core Ops, SparseCore 0:
  9.5 47.8 all-gather.29
  60.2 40.0 all-gather.11
  102.4 40.0 all-gather.13
  145.3 40.0 all-gather.15
  187.4 40.0 all-gather.17
  230.3 40.0 all-gather.19
  272.5 40.0 all-gather.21
  315.4 40.0 all-gather.23
  357.7 40.0 all-gather.25
  400.5 40.0 all-gather.27
where the time goes:
time: 451 us; the launch traced here: 450 us
  waiting for transfers between devices  392 us (87%)
  matrix products  28.9 us (6%)
  between operations  13.7 us (3%)
  starting transfers between devices  11.9 us (3%)
    all_gather x5, waiting for transfers between devices, combine(): lax.all_gather(maps, 'space', axis=0, tiled=True)  200 us
    all_gather x5, waiting for transfers between devices, combine(): lax.all_gather(weighted, 'space', axis=0, tiled=True)  170 us
    ppermute x9, waiting for transfers between devices, from_behind(): return lax.ppermute(shard, axis, pairs)  21.6 us
    dot_general x9, matrix products, matmul(): jnp.dot(left, right, precision=HIGH, preferred_element_type=jnp.float32)  18.4 us
    ppermute x9, starting transfers between devices, from_behind(): return lax.ppermute(shard, axis, pairs)  11.6 us
    dot_general x5, matrix products, inner_rows(): lax.dot_general(left, right, (((0,), (0,)), ((), ())), precision=HIGH, pr...  10.5 us
  transfers between devices with their start and end apart: 19, of which 15 were waited for; matrix products, arithmetic and copies ran while one was open for 3% of the time, Pallas kernels for 0%

commit v1 on v0

--- a/solution.py
+++ b/solution.py
@@ -33,9 +33,10 @@
 
     folded = accumulate(lax.all_gather(maps, "space", axis=0, tiled=True))
     weighted = folded[0]
-    own_columns = lax.dynamic_slice_in_dim(
-        lax.all_gather(maps, "space", axis=0, tiled=True), owner * rows, rows, 1
+    wrap_local_data = lambda raw: jnp.concatenate(
+        lax.all_to_all(jnp.stack([raw for _ in range(lax.psum(1, "space"))]), "space", 0, 0), axis=0
     )
+    own_columns = lax.dynamic_slice_in_dim(wrap_local_data(maps), owner * rows, rows, 1)
     congruence = inner_rows(own_columns, lax.all_gather(weighted, "space", axis=0, tiled=True))
     new_terms = terms + congruence
     new_maps = None if later_maps is None else folded[1]

time: 451 us -> 487 us (1.080)
  starting transfers between devices: 11.9 us -> 34.9 us
  waiting for transfers between devices: 392 us -> 399 us
  local copies, waits for them, and re-layouts: 3.15 us -> 8.93 us
    all_to_all x0 -> x5, waiting for transfers between devices: none -> 92.4 us  [combine(): lax.all_to_all(jnp.stack([raw for _ in range(lax.psum(1, 'space'))]), 'sp...]
    all_gather x5, waiting for transfers between devices: 170 us -> 81.7 us  [combine(): lax.all_gather(weighted, 'space', axis=0, tiled=True)]
    all_to_all x0 -> x5, starting transfers between devices: none -> 23 us  [combine(): lax.all_to_all(jnp.stack([raw for _ in range(lax.psum(1, 'space'))]), 'sp...]
    another operation x0 -> x5, local copies, waits for them, and re-layouts: none -> 5.58 us  [combine(): jnp.stack([raw for _ in range(lax.psum(1, 'space'))])]
  transfers between devices with their start and end apart: 19 -> 24, of which waited for: 15 -> 19; matrix products, arithmetic and copies ran while one was open for 3% -> 4% of each run, Pallas kernels for 0% -> 0%
where the time goes in v1:
time: 487 us; the launch traced here: 486 us
  waiting for transfers between devices  399 us (82%)
  starting transfers between devices  34.9 us (7%)
  matrix products  28.6 us (6%)
  between operations  13.7 us (3%)
  local copies, waits for them, and re-layouts  8.93 us (2%)
    all_gather x5, waiting for transfers between devices, combine(): folded = accumulate(lax.all_gather(maps, 'space', axis=0, tiled=True))  201 us
    all_to_all x5, waiting for transfers between devices, combine(): lax.all_to_all(jnp.stack([raw for _ in range(lax.psum(1, 'space'))]), 'sp...  92.4 us
    all_gather x5, waiting for transfers between devices, combine(): lax.all_gather(weighted, 'space', axis=0, tiled=True)  81.7 us
    ppermute x9, waiting for transfers between devices, from_behind(): return lax.ppermute(shard, axis, pairs)  23.7 us
    all_to_all x5, starting transfers between devices, combine(): lax.all_to_all(jnp.stack([raw for _ in range(lax.psum(1, 'space'))]), 'sp...  23 us
    dot_general x9, matrix products, matmul(): jnp.dot(left, right, precision=HIGH, preferred_element_type=jnp.float32)  18.1 us
    ppermute x9, starting transfers between devices, from_behind(): return lax.ppermute(shard, axis, pairs)  11.6 us
    dot_general x5, matrix products, inner_rows(): lax.dot_general(left, right, (((0,), (0,)), ((), ())), precision=HIGH, pr...  10.4 us
  transfers between devices with their start and end apart: 24, of which 19 were waited for; matrix products, arithmetic and copies ran while one was open for 4% of the time, Pallas kernels for 0%

profile of v1, /device:TPU:1, one launch (start us, length us, event | category | flops | bytes accessed | tf_op | source)
XLA Modules:
  0.0 485.6 jit_solution(15103898753872579437)
XLA Ops:
  8.7 4.3 collective-permute-done
  13.0 44.4 %all-gather.30.cloned.1.call-done = f32[1,512,512]{2,1,0:T(8,128)} async-done(((f32[1,32,512]{2,1,0:T(8,128)}), f32[1,512,512]{2,1,0:T(8,128)}) %all-gather.30.cloned.1.call-update) | async-done | bytes 1048592 | tf_op jit(solution)/shard_map/all_gather | solution.py:34
  61.9 4.6 all-to-all-start
  67.8 4.3 collective-permute-done.1
  73.5 23.7 %all-to-all-done = f32[16,32,512]{2,1,0:T(8,128)S(1)} async-done(((f32[16,32,512]{2,1,0:T(8,128)}), f32[16,32,512]{2,1,0:T(8,128)S(1)}, u32[]{:S(2)}, u32[]{:S(2)}) %all-to-all-start) | async-done | bytes 1048608 | tf_op jit(solution)/shard_map/all_to_all | solution.py:37
  97.2 9.5 %all-gather.12.cloned.1.call-done = f32[512,512]{1,0:T(8,128)} async-done(((f32[32,512]{1,0:T(8,128)}), f32[512,512]{1,0:T(8,128)}) %all-gather.12.cloned.1.call-update) | async-done | bytes 1048592 | tf_op jit(solution)/shard_map/all_gather | solution.py:40
  110.0 39.3 %all-gather.14.cloned.1.call-done = f32[512,512]{1,0:T(8,128)} async-done(((f32[32,512]{1,0:T(8,128)}), f32[512,512]{1,0:T(8,128)}) %all-gather.14.cloned.1.call-update) | async-done | bytes 1048592 | tf_op jit(solution)/shard_map/all_gather | solution.py:34
  153.8 4.6 all-to-all-start.1
  159.7 5.8 %collective-permute-done.3 = f32[32,512]{1,0:T(8,128)S(1)} collective-permute-done((f32[32,512]{1,0:T(8,128)S(1)}, f32[32,512]{1,0:T(8,128)S(1)}, u32[]{:S(2)}, u32[]{:S(2)}) %collective-permute-start.3) | collective-permute-done | bytes 65568 | tf_op jit(solution)/shard_map/ppermute | solution.py:12
  166.9 22.2 %all-to-all-done.1 = f32[16,32,512]{2,1,0:T(8,128)S(1)} async-done(((f32[16,32,512]{2,1,0:T(8,128)}), f32[16,32,512]{2,1,0:T(8,128)S(1)}, u32[]{:S(2)}, u32[]{:S(2)}) %all-to-all-start.1) | async-done | bytes 1048608 | tf_op jit(solution)/shard_map/all_to_all | solution.py:37
  189.1 9.5 %all-gather.16.cloned.1.call-done = f32[512,512]{1,0:T(8,128)} async-done(((f32[32,512]{1,0:T(8,128)}), f32[512,512]{1,0:T(8,128)}) %all-gather.16.cloned.1.call-update) | async-done | bytes 1048592 | tf_op jit(solution)/shard_map/all_gather | solution.py:40
  201.9 39.2 %all-gather.18.cloned.1.call-done = f32[512,512]{1,0:T(8,128)} async-done(((f32[32,512]{1,0:T(8,128)}), f32[512,512]{1,0:T(8,128)}) %all-gather.18.cloned.1.call-update) | async-done | bytes 1048592 | tf_op jit(solution)/shard_map/all_gather | solution.py:34
  245.5 4.6 all-to-all-start.2
  251.5 4.3 collective-permute-done.5
  257.1 23.7 %all-to-all-done.2 = f32[16,32,512]{2,1,0:T(8,128)S(1)} async-done(((f32[16,32,512]{2,1,0:T(8,128)}), f32[16,32,512]{2,1,0:T(8,128)S(1)}, u32[]{:S(2)}, u32[]{:S(2)}) %all-to-all-start.2) | async-done | bytes 1048608 | tf_op jit(solution)/shard_map/all_to_all | solution.py:37
  280.8 9.5 %all-gather.20.cloned.1.call-done = f32[512,512]{1,0:T(8,128)} async-done(((f32[32,512]{1,0:T(8,128)}), f32[512,512]{1,0:T(8,128)}) %all-gather.20.cloned.1.call-update) | async-done | bytes 1048592 | tf_op jit(solution)/shard_map/all_gather | solution.py:40
  293.6 39.3 %all-gather.22.cloned.1.call-done = f32[512,512]{1,0:T(8,128)} async-done(((f32[32,512]{1,0:T(8,128)}), f32[512,512]{1,0:T(8,128)}) %all-gather.22.cloned.1.call-update) | async-done | bytes 1048592 | tf_op jit(solution)/shard_map/all_gather | solution.py:34
  337.4 4.6 all-to-all-start.3
  343.4 5.2 %collective-permute-done.7 = f32[32,512]{1,0:T(8,128)S(1)} collective-permute-done((f32[32,512]{1,0:T(8,128)S(1)}, f32[32,512]{1,0:T(8,128)S(1)}, u32[]{:S(2)}, u32[]{:S(2)}) %collective-permute-start.7) | collective-permute-done | bytes 65568 | tf_op jit(solution)/shard_map/ppermute | solution.py:12
  349.9 22.8 %all-to-all-done.3 = f32[16,32,512]{2,1,0:T(8,128)S(1)} async-done(((f32[16,32,512]{2,1,0:T(8,128)}), f32[16,32,512]{2,1,0:T(8,128)S(1)}, u32[]{:S(2)}, u32[]{:S(2)}) %all-to-all-start.3) | async-done | bytes 1048608 | tf_op jit(solution)/shard_map/all_to_all | solution.py:37
  372.7 9.5 %all-gather.24.cloned.1.call-done = f32[512,512]{1,0:T(8,128)} async-done(((f32[32,512]{1,0:T(8,128)}), f32[512,512]{1,0:T(8,128)}) %all-gather.24.cloned.1.call-update) | async-done | bytes 1048592 | tf_op jit(solution)/shard_map/all_gather | solution.py:40
  386.7 4.6 all-to-all-start.4
  391.3 38.5 %all-gather.26.cloned.1.call-done = f32[512,512]{1,0:T(8,128)} async-done(((f32[32,512]{1,0:T(8,128)}), f32[512,512]{1,0:T(8,128)}) %all-gather.26.cloned.1.call-update) | async-done | bytes 1048592 | tf_op jit(solution)/shard_map/all_gather | solution.py:34
  432.5 43.7 %all-gather.28.cloned.1.call-done = f32[512,512]{1,0:T(8,128)} async-done(((f32[32,512]{1,0:T(8,128)}), f32[512,512]{1,0:T(8,128)}) %all-gather.28.cloned.1.call-update) | async-done | bytes 1048592 | tf_op jit(solution)/shard_map/all_gather | solution.py:40
  (73 shorter events, 50.4 us)
Async XLA Ops:
  6.5 50.8 %all-gather.30.cloned.1.call-start = ((), (), s32[]{:S(2)}) async-start(), calls=%async_computation.14 | async-start | bytes 1114112 | tf_op jit(solution)/shard_map/all_gather | solution.py:34
  7.3 99.4 %all-gather.12.cloned.1.call-start = ((), (), s32[]{:S(2)}) async-start(), calls=%async_computation.5 | async-start | bytes 1114112 | tf_op jit(solution)/shard_map/all_gather | solution.py:40
  7.4 5.6 %collective-permute-start = (f32[32,512]{1,0:T(8,128)S(1)}, f32[32,512]{1,0:T(8,128)S(1)}, u32[]{:S(2)}, u32[]{:S(2)}) collective-permute-start(f32[32,512]{1,0:T(8,128)S(1)} %bitcast.43), channel_id=1, source_target_pairs={{16,0},{32,16},{48,32},{64,48},{80,64},{96,80},{112,96},{128,112},... | collective-permute-start | bytes 196616 | tf_op jit(solution)/shard_map/ppermute | solution.py:12
  61.9 35.3 %all-to-all-start = ((f32[16,32,512]{2,1,0:T(8,128)}), f32[16,32,512]{2,1,0:T(8,128)S(1)}, u32[]{:S(2)}, u32[]{:S(2)}) async-start(f32[16,32,512]{2,1,0:T(8,128)} %stack.10), calls=%async_computation | async-start | bytes 2097152 | tf_op jit(solution)/shard_map/all_to_all | solution.py:37
  66.5 82.8 %all-gather.14.cloned.1.call-start = ((), (), s32[]{:S(2)}) async-start(), calls=%async_computation.6 | async-start | bytes 1114112 | tf_op jit(solution)/shard_map/all_gather | solution.py:34
  66.5 5.6 %collective-permute-start.1 = (f32[32,512]{1,0:T(8,128)S(1)}, f32[32,512]{1,0:T(8,128)S(1)}, u32[]{:S(2)}, u32[]{:S(2)}) collective-permute-start(f32[32,512]{1,0:T(8,128)S(1)} %bitcast.42), channel_id=1, source_target_pairs={{16,0},{32,16},{48,32},{64,48},{80,64},{96,80},{112,96},{128,112},... | collective-permute-start | bytes 196616 | tf_op jit(solution)/shard_map/ppermute | solution.py:12
  73.4 125.2 %all-gather.16.cloned.1.call-start = ((), (), s32[]{:S(2)}) async-start(), calls=%async_computation.7 | async-start | bytes 1114112 | tf_op jit(solution)/shard_map/all_gather | solution.py:40
  108.7 40.6 %collective-permute-start.2 = (f32[32,512]{1,0:T(8,128)S(1)}, f32[32,512]{1,0:T(8,128)S(1)}, u32[]{:S(2)}, u32[]{:S(2)}) collective-permute-start(f32[32,512]{1,0:T(8,128)S(1)} %convolution_add_fusion.4), channel_id=1, source_target_pairs={{32,0},{48,16},{64,32},{80,48},{96,64},{112,80},{128,96},{144,112}... | collective-permute-start | bytes 196616 | tf_op jit(solution)/shard_map/ppermute | solution.py:12
  153.8 35.3 %all-to-all-start.1 = ((f32[16,32,512]{2,1,0:T(8,128)}), f32[16,32,512]{2,1,0:T(8,128)S(1)}, u32[]{:S(2)}, u32[]{:S(2)}) async-start(f32[16,32,512]{2,1,0:T(8,128)} %stack.11), calls=%async_computation.1 | async-start | bytes 2097152 | tf_op jit(solution)/shard_map/all_to_all | solution.py:37
  158.4 82.6 %all-gather.18.cloned.1.call-start = ((), (), s32[]{:S(2)}) async-start(), calls=%async_computation.8 | async-start | bytes 1114112 | tf_op jit(solution)/shard_map/all_gather | solution.py:34
  158.4 7.1 %collective-permute-start.3 = (f32[32,512]{1,0:T(8,128)S(1)}, f32[32,512]{1,0:T(8,128)S(1)}, u32[]{:S(2)}, u32[]{:S(2)}) collective-permute-start(f32[32,512]{1,0:T(8,128)S(1)} %copy-done.4), channel_id=1, source_target_pairs={{32,0},{48,16},{64,32},{80,48},{96,64},{112,80},{128,96},{144,112}... | collective-permute-start | bytes 196616 | tf_op jit(solution)/shard_map/ppermute | solution.py:12
  166.8 123.5 %all-gather.20.cloned.1.call-start = ((), (), s32[]{:S(2)}) async-start(), calls=%async_computation.9 | async-start | bytes 1114112 | tf_op jit(solution)/shard_map/all_gather | solution.py:40
  200.6 40.5 %collective-permute-start.4 = (f32[32,512]{1,0:T(8,128)S(1)}, f32[32,512]{1,0:T(8,128)S(1)}, u32[]{:S(2)}, u32[]{:S(2)}) collective-permute-start(f32[32,512]{1,0:T(8,128)S(1)} %convolution_add_fusion.3), channel_id=1, source_target_pairs={{64,0},{80,16},{96,32},{112,48},{128,64},{144,80},{160,96},{176,11... | collective-permute-start | bytes 196616 | tf_op jit(solution)/shard_map/ppermute | solution.py:12
  245.5 35.3 %all-to-all-start.2 = ((f32[16,32,512]{2,1,0:T(8,128)}), f32[16,32,512]{2,1,0:T(8,128)S(1)}, u32[]{:S(2)}, u32[]{:S(2)}) async-start(f32[16,32,512]{2,1,0:T(8,128)} %stack.12), calls=%async_computation.2 | async-start | bytes 2097152 | tf_op jit(solution)/shard_map/all_to_all | solution.py:37
  250.1 82.8 %all-gather.22.cloned.1.call-start = ((), (), s32[]{:S(2)}) async-start(), calls=%async_computation.10 | async-start | bytes 1114112 | tf_op jit(solution)/shard_map/all_gather | solution.py:34
  250.2 5.6 %collective-permute-start.5 = (f32[32,512]{1,0:T(8,128)S(1)}, f32[32,512]{1,0:T(8,128)S(1)}, u32[]{:S(2)}, u32[]{:S(2)}) collective-permute-start(f32[32,512]{1,0:T(8,128)S(1)} %copy-done.5), channel_id=1, source_target_pairs={{64,0},{80,16},{96,32},{112,48},{128,64},{144,80},{160,96},{176,11... | collective-permute-start | bytes 196616 | tf_op jit(solution)/shard_map/ppermute | solution.py:12
  257.1 125.1 %all-gather.24.cloned.1.call-start = ((), (), s32[]{:S(2)}) async-start(), calls=%async_computation.11 | async-start | bytes 1114112 | tf_op jit(solution)/shard_map/all_gather | solution.py:40
  292.3 40.6 %collective-permute-start.6 = (f32[32,512]{1,0:T(8,128)S(1)}, f32[32,512]{1,0:T(8,128)S(1)}, u32[]{:S(2)}, u32[]{:S(2)}) collective-permute-start(f32[32,512]{1,0:T(8,128)S(1)} %convolution_add_fusion.2), channel_id=1, source_target_pairs={{128,0},{144,16},{160,32},{176,48},{192,64},{208,80},{224,96},{240... | collective-permute-start | bytes 196616 | tf_op jit(solution)/shard_map/ppermute | solution.py:12
  337.4 35.3 %all-to-all-start.3 = ((f32[16,32,512]{2,1,0:T(8,128)}), f32[16,32,512]{2,1,0:T(8,128)S(1)}, u32[]{:S(2)}, u32[]{:S(2)}) async-start(f32[16,32,512]{2,1,0:T(8,128)} %stack.13), calls=%async_computation.3 | async-start | bytes 2097152 | tf_op jit(solution)/shard_map/all_to_all | solution.py:37
  342.0 87.9 %all-gather.26.cloned.1.call-start = ((), (), s32[]{:S(2)}) async-start(), calls=%async_computation.12 | async-start | bytes 1114112 | tf_op jit(solution)/shard_map/all_gather | solution.py:34
  342.1 6.5 %collective-permute-start.7 = (f32[32,512]{1,0:T(8,128)S(1)}, f32[32,512]{1,0:T(8,128)S(1)}, u32[]{:S(2)}, u32[]{:S(2)}) collective-permute-start(f32[32,512]{1,0:T(8,128)S(1)} %copy-done.6), channel_id=1, source_target_pairs={{128,0},{144,16},{160,32},{176,48},{192,64},{208,80},{224,96},{240... | collective-permute-start | bytes 196616 | tf_op jit(solution)/shard_map/ppermute | solution.py:12
  384.2 45.6 %collective-permute-start.8 = (f32[32,512]{1,0:T(8,128)S(1)}, f32[32,512]{1,0:T(8,128)S(1)}, u32[]{:S(2)}, u32[]{:S(2)}) collective-permute-start(f32[32,512]{1,0:T(8,128)S(1)} %convolution_add_fusion.1), channel_id=1, source_target_pairs={{256,0},{272,16},{288,32},{304,48},{320,64},{336,80},{352,96},{368... | collective-permute-start | bytes 196616 | tf_op jit(solution)/shard_map/ppermute | solution.py:12
  386.7 45.8 %all-to-all-start.4 = ((f32[16,32,512]{2,1,0:T(8,128)}), f32[16,32,512]{2,1,0:T(8,128)S(1)}, u32[]{:S(2)}, u32[]{:S(2)}) async-start(f32[16,32,512]{2,1,0:T(8,128)} %stack.14), calls=%async_computation.4 | async-start | bytes 2097152 | tf_op jit(solution)/shard_map/all_to_all | solution.py:37
  391.3 84.9 %all-gather.28.cloned.1.call-start = ((), (), s32[]{:S(2)}) async-start(), calls=%async_computation.13 | async-start | bytes 1114112 | tf_op jit(solution)/shard_map/all_gather | solution.py:40
  (10 other events, 50.7 us)
Sparse Core Ops, SparseCore 0:
  9.5 47.8 all-gather.29
  60.1 46.5 all-gather.11
  108.8 40.3 all-gather.13
  152.0 46.5 all-gather.15
  200.6 40.4 all-gather.17
  243.7 46.5 all-gather.19
  292.5 40.4 all-gather.21
  335.6 46.5 all-gather.23
  384.4 45.4 all-gather.25
  432.6 43.5 all-gather.27
